TPU v7x, 512 devices: a whole 4x4x16 slice. The times are simulated.
512 devices in a mesh: blk: 64 (over x, y, z_hi, core), ulysses: 8 (over z_lo).
Axes of the slice: x: 4, y: 4, z: 16 (z_hi: 2, z_lo: 8; z = z_hi * 8 + z_lo), core: 2. Of those that a mesh axis runs over, the one named last changes fastest.
Arguments:
- query_rows: bfloat16 [8192, 3072], P('blk', 'ulysses'), may hold values from -8 to 8
- key_rows: bfloat16 [8192, 3072], P('blk', 'ulysses'), may hold values from -8 to 8
- value_rows: bfloat16 [8192, 3072], P('blk', 'ulysses'), may hold values from -6 to 6
Outputs:
- attended: bfloat16 [8192, 3072], P(('blk', 'ulysses'))
All inputs are finite; a program needn't handle non-finite values.
Results may differ from a plain program's by a relative error of at most 0.0055.
Values may be sent and summed in bfloat16 or wider, within the bound.
A program may use at most 128 MiB of HBM per device.

v0:
```python
import math

import jax
import jax.numpy as jnp
from jax import lax
from jax.sharding import PartitionSpec as P

HD = 128


def from_partner(value, axis, bit):
    mask = 2**bit
    pairs = [(source, source ^ mask) for source in range(lax.axis_size(axis))]
    return lax.ppermute(value, axis, pairs)


def block_scores(query_heads, key_block, head_count):
    key_heads = key_block.reshape(key_block.shape[0], head_count, HD)
    return jnp.einsum(
        "rhd,khd->rhk", query_heads, key_heads, preferred_element_type=jnp.float32
    ) * HD ** (-0.5)


def absorb_block(running, key_block, value_block, query_heads, head_count):
    run_peak, run_total, run_sums = running
    value_heads = value_block.reshape(value_block.shape[0], head_count, HD)
    scores = block_scores(query_heads, key_block, head_count)
    new_peak = jnp.maximum(run_peak, jnp.max(scores, axis=2))
    fading = jnp.exp(run_peak - new_peak)
    raised = jnp.exp(scores - new_peak[:, :, None])
    new_total = run_total * fading + jnp.sum(raised, axis=2)
    weights = raised.astype(jnp.bfloat16)
    new_sums = run_sums * fading[:, :, None] + jnp.einsum(
        "rhk,khd->rhd", weights, value_heads, preferred_element_type=jnp.float32
    )
    return (new_peak, new_total, new_sums)


def split_blocks(matrix):
    piece_rows = matrix.shape[0]
    block_rows = math.gcd(piece_rows, 512)
    return matrix.reshape(piece_rows // block_rows, block_rows, matrix.shape[1])


def on_device(query_rows, key_rows, value_rows):
    head_count = query_rows.shape[1] // HD
    query_count = query_rows.shape[0]
    query_heads = query_rows.reshape(query_count, head_count, HD)
    start_total = jnp.zeros((query_count, head_count), jnp.float32)
    start_sums = jnp.zeros((query_count, head_count, HD), jnp.float32)
    levels = lax.axis_size("blk").bit_length() - 1

    def fold_piece(running, key_piece, value_piece):

        def advance(state_now, blocks_pair):
            return (
                absorb_block(state_now, blocks_pair[0], blocks_pair[1], query_heads, head_count),
                None,
            )

        finished, unused = lax.scan(
            advance, running, (split_blocks(key_piece), split_blocks(value_piece))
        )
        return finished

    start_peak = jnp.full((query_count, head_count), -1e30, jnp.float32)
    running = fold_piece((start_peak, start_total, start_sums), key_rows, value_rows)
    held_keys, held_values = (key_rows, value_rows)
    for bit in range(levels):
        other_keys, other_values = from_partner((held_keys, held_values), "blk", bit)
        running = fold_piece(running, other_keys, other_values)
        if bit + 1 < levels:
            held_keys = jnp.concatenate([held_keys, other_keys], axis=0)
            held_values = jnp.concatenate([held_values, other_values], axis=0)
    total, sums = (running[1], running[2])
    attended = (sums / total[:, :, None]).astype(jnp.bfloat16).reshape(query_count, head_count * HD)
    return lax.all_to_all(attended, "ulysses", split_axis=0, concat_axis=1, tiled=True)


def solution(mesh):
    return jax.shard_map(
        on_device,
        mesh=mesh,
        in_specs=(P("blk", "ulysses"), P("blk", "ulysses"), P("blk", "ulysses")),
        out_specs=P(("blk", "ulysses"), None),
        check_vma=False,
    )
```

profile of v0, /device:TPU:1, one launch (start us, length us, event | category | flops | bytes accessed | tf_op | source)
XLA Modules:
  0.0 375.0 jit_solution(12495869390898863407)
XLA Ops:
  0.0 1.0 copy.89
  1.0 8.8 %collective-permute-start.3 = (bf16[128,384]{0,1:T(8,128)(2,1)S(1)}, bf16[128,384]{0,1:T(8,128)(2,1)S(1)}, u32[]{:S(2)}, u32[]{:S(2)}) collective-permute-start(bf16[128,384]{0,1:T(8,128)(2,1)S(1)} %copy.89), channel_id=1, source_target_pairs={{0,8},{8,0},{16,24},{24,16},{32,40},{40,32},{48,56},{56,48},{64,72... | collective-permute-start | bytes 294920 | tf_op jit(solution)/shard_map/ppermute | solution.py:14
  9.8 1.0 copy.76
  10.8 1.9 collective-permute-start
  12.8 0.7 constant_dynamic-update-slice_fusion.21
  13.5 1.0 copy.77
  14.9 0.7 constant_dynamic-update-slice_fusion.15
  15.9 10.1 %collective-permute-start.4 = (bf16[256,384]{0,1:T(8,128)(2,1)S(1)}, bf16[256,384]{0,1:T(8,128)(2,1)S(1)}, u32[]{:S(2)}, u32[]{:S(2)}) collective-permute-start(bf16[256,384]{0,1:T(8,128)(2,1)S(1)} %pad_maximum_fusion.5), channel_id=1, source_target_pairs={{0,16},{8,24},{16,0},{24,8},{32,48},{40,56},{48,32},{56,40},{64,80... | collective-permute-start | bytes 589832 | tf_op jit(solution)/shard_map/ppermute | solution.py:14
  26.0 3.9 %collective-permute-start.1 = (bf16[256,384]{0,1:T(8,128)(2,1)S(1)}, bf16[256,384]{0,1:T(8,128)(2,1)S(1)}, u32[]{:S(2)}, u32[]{:S(2)}) collective-permute-start(bf16[256,384]{0,1:T(8,128)(2,1)S(1)} %pad_maximum_fusion.4), channel_id=1, source_target_pairs={{0,16},{8,24},{16,0},{24,8},{32,48},{40,56},{48,32},{56,40},{64,80... | collective-permute-start | bytes 589832 | tf_op jit(solution)/shard_map/ppermute | solution.py:14
  29.9 0.8 constant_dynamic-update-slice_fusion.20
  30.7 0.7 constant_dynamic-update-slice_fusion.14
  31.4 1.2 collective-permute-done.4
  32.7 1.9 collective-permute-start.5
  34.6 8.3 %collective-permute-done.1 = bf16[256,384]{0,1:T(8,128)(2,1)S(1)} collective-permute-done((bf16[256,384]{0,1:T(8,128)(2,1)S(1)}, bf16[256,384]{0,1:T(8,128)(2,1)S(1)}, u32[]{:S(2)}, u32[]{:S(2)}) %collective-permute-start.1) | collective-permute-done | bytes 196640 | tf_op jit(solution)/shard_map/ppermute | solution.py:14
  42.9 10.5 %collective-permute-start.2 = (bf16[512,384]{0,1:T(8,128)(2,1)S(1)}, bf16[512,384]{0,1:T(8,128)(2,1)S(1)}, u32[]{:S(2)}, u32[]{:S(2)}) collective-permute-start(bf16[512,384]{0,1:T(8,128)(2,1)S(1)} %pad_maximum_fusion.2), channel_id=1, source_target_pairs={{0,32},{8,40},{16,48},{24,56},{32,0},{40,8},{48,16},{56,24},{64,96... | collective-permute-start | bytes 1179656 | tf_op jit(solution)/shard_map/ppermute | solution.py:14
  53.4 0.8 constant_dynamic-update-slice_fusion.19
  54.2 0.9 constant_dynamic-update-slice_fusion.13
  55.4 5.5 %collective-permute-done.2 = bf16[512,384]{0,1:T(8,128)(2,1)S(1)} collective-permute-done((bf16[512,384]{0,1:T(8,128)(2,1)S(1)}, bf16[512,384]{0,1:T(8,128)(2,1)S(1)}, u32[]{:S(2)}, u32[]{:S(2)}) %collective-permute-start.2) | collective-permute-done | bytes 393248 | tf_op jit(solution)/shard_map/ppermute | solution.py:14
  61.6 1.0 pad_maximum_fusion.1
  62.6 4.7 %collective-permute-start.7 = (bf16[1024,384]{0,1:T(8,128)(2,1)}, bf16[1024,384]{0,1:T(8,128)(2,1)S(1)}, u32[]{:S(2)}, u32[]{:S(2)}) collective-permute-start(bf16[1024,384]{0,1:T(8,128)(2,1)} %pad_maximum_fusion.1), channel_id=1, source_target_pairs={{0,64},{8,72},{16,80},{24,88},{32,96},{40,104},{48,112},{56,120},{... | collective-permute-start | bytes 2359304 | tf_op jit(solution)/shard_map/ppermute | solution.py:14
  67.3 1.0 pad_maximum_fusion
  68.3 2.1 collective-permute-start.6
  71.6 1.0 constant_dynamic-update-slice_fusion.18
  72.6 1.0 constant_dynamic-update-slice_fusion.12
  73.6 25.8 %collective-permute-done.6 = bf16[1024,384]{0,1:T(8,128)(2,1)S(1)} collective-permute-done((bf16[1024,384]{0,1:T(8,128)(2,1)}, bf16[1024,384]{0,1:T(8,128)(2,1)S(1)}, u32[]{:S(2)}, u32[]{:S(2)}) %collective-permute-start.6) | collective-permute-done | bytes 786464 | tf_op jit(solution)/shard_map/ppermute | solution.py:14
  99.5 1.4 constant_dynamic-update-slice_fusion.17
  100.9 2.7 collective-permute-start.9
  103.6 1.4 constant_dynamic-update-slice_fusion.11
  105.0 2.6 collective-permute-start.8
  108.0 2.3 while.6
  110.3 25.2 %collective-permute-done.9 = bf16[2048,384]{0,1:T(8,128)(2,1)} collective-permute-done((bf16[2048,384]{0,1:T(8,128)(2,1)}, bf16[2048,384]{0,1:T(8,128)(2,1)}, u32[]{:S(2)}, u32[]{:S(2)}) %collective-permute-start.9) | collective-permute-done | bytes 1572896 | tf_op jit(solution)/shard_map/ppermute | solution.py:14
  135.5 2.8 constant_dynamic-update-slice_fusion.16
  138.3 3.9 %collective-permute-start.11 = (bf16[4096,384]{0,1:T(8,128)(2,1)}, bf16[4096,384]{0,1:T(8,128)(2,1)}, u32[]{:S(2)}, u32[]{:S(2)}) collective-permute-start(bf16[4096,384]{0,1:T(8,128)(2,1)} %constant_dynamic-update-slice_fusion.16), channel_id=1, source_target_pairs={{0,256},{8,264},{16,272},{24,280},{32,288},{40,296},{48,304},{56,3... | collective-permute-start | bytes 9437192 | tf_op jit(solution)/shard_map/ppermute | solution.py:14
  142.2 27.0 %collective-permute-done.8 = bf16[2048,384]{0,1:T(8,128)(2,1)} collective-permute-done((bf16[2048,384]{0,1:T(8,128)(2,1)}, bf16[2048,384]{0,1:T(8,128)(2,1)}, u32[]{:S(2)}, u32[]{:S(2)}) %collective-permute-start.8) | collective-permute-done | bytes 1572896 | tf_op jit(solution)/shard_map/ppermute | solution.py:14
  169.2 1.5 copy.155
  170.7 2.8 constant_dynamic-update-slice_fusion.10
  173.5 3.9 %collective-permute-start.10 = (bf16[4096,384]{0,1:T(8,128)(2,1)}, bf16[4096,384]{0,1:T(8,128)(2,1)}, u32[]{:S(2)}, u32[]{:S(2)}) collective-permute-start(bf16[4096,384]{0,1:T(8,128)(2,1)} %constant_dynamic-update-slice_fusion.10), channel_id=1, source_target_pairs={{0,256},{8,264},{16,272},{24,280},{32,288},{40,296},{48,304},{56,3... | collective-permute-start | bytes 9437192 | tf_op jit(solution)/shard_map/ppermute | solution.py:14
  177.5 2.6 copy.110
  180.1 8.5 %while.7 = (s32[]{:T(128)}, f32[128,3]{0,1:T(4,128)S(1)}, f32[128,3]{0,1:T(4,128)S(1)}, f32[128,3,128]{0,2,1:T(8,128)S(1)}, bf16[4,512,384]{1,2,0:T(8,128)(2,1)S...) while((s32[]{:T(128)}, f32[128,3]{0,1:T(4,128)S(1)}, ...), condition=%wide.region_15.16_spmd, body=%wide.region_12.15_spmd.sunk | while | flops 101942016 | bytes 6021221 | solution.py:61
  180.1 1.0 constant_dynamic-slice_fusion.15
  182.2 1.0 constant_dynamic-slice_fusion.15
  184.3 1.0 constant_dynamic-slice_fusion.15
  186.5 1.0 constant_dynamic-slice_fusion.15
  188.6 116.9 %collective-permute-done.10 = bf16[4096,384]{0,1:T(8,128)(2,1)} collective-permute-done((bf16[4096,384]{0,1:T(8,128)(2,1)}, bf16[4096,384]{0,1:T(8,128)(2,1)}, u32[]{:S(2)}, u32[]{:S(2)}) %collective-permute-start.10) | collective-permute-done | bytes 3145760 | tf_op jit(solution)/shard_map/ppermute | solution.py:14
  305.5 3.9 %copy.154 = bf16[48,8,8,512]{3,2,0,1:T(8,128)(2,1)} copy(bf16[48,8,8,512]{3,2,1,0:T(8,128)(2,1)} %bitcast.37) | data formatting | bytes 6291456 | tf_op jit(solution)/shard_map/reshape | solution.py:42
  309.4 4.7 %copy.116 = bf16[4096,384]{1,0:T(8,128)(2,1)} copy(bf16[4096,384]{0,1:T(8,128)(2,1)} %collective-permute-done.11) | data formatting | bytes 6291456 | tf_op jit(solution)/shard_map/ppermute | solution.py:14
  314.1 25.0 %while.8 = (s32[]{:T(128)}, f32[128,3]{0,1:T(4,128)S(1)}, f32[128,3]{0,1:T(4,128)S(1)}, f32[128,3,128]{0,2,1:T(8,128)S(1)}, bf16[8,512,384]{1,2,0:T(8,128)(2,1)}...) while((s32[]{:T(128)}, f32[128,3]{0,1:T(4,128)S(1)}, ...), condition=%wide.region_19.20_spmd, body=%wide.region_16.19_spmd.sunk | while | flops 101942016 | bytes 6021221 | solution.py:61
  314.1 1.0 constant_dynamic-slice_fusion.17
  315.3 1.0 constant_dynamic-slice_fusion.16
  317.2 1.0 constant_dynamic-slice_fusion.17
  318.4 1.0 constant_dynamic-slice_fusion.16
  320.3 1.0 constant_dynamic-slice_fusion.17
  321.6 1.0 constant_dynamic-slice_fusion.16
  323.5 1.0 constant_dynamic-slice_fusion.17
  324.7 1.0 constant_dynamic-slice_fusion.16
  326.6 1.0 constant_dynamic-slice_fusion.17
  327.8 1.0 constant_dynamic-slice_fusion.16
  329.7 1.0 constant_dynamic-slice_fusion.17
  330.9 1.0 constant_dynamic-slice_fusion.16
  332.8 1.0 constant_dynamic-slice_fusion.17
  334.1 1.0 constant_dynamic-slice_fusion.16
  336.0 1.0 constant_dynamic-slice_fusion.17
  337.2 1.0 constant_dynamic-slice_fusion.16
  339.3 35.0 %all_to_all.19 = bf16[8,16,384]{2,1,0:T(8,128)(2,1)S(1)} all-to-all(bf16[8,16,384]{2,1,0:T(8,128)(2,1)S(1)} %all_to_all.14), channel_id=1, replica_groups=mesh['blk'=64,'ulysses'=8] {'ulysses'}, dimensions={0} | all-to-all | bytes 196608 | tf_op jit(solution)/shard_map/all_to_all | solution.py:77
  (136 shorter events, 18.5 us)
Async XLA Ops:
  1.0 14.9 %collective-permute-start.3 = (bf16[128,384]{0,1:T(8,128)(2,1)S(1)}, bf16[128,384]{0,1:T(8,128)(2,1)S(1)}, u32[]{:S(2)}, u32[]{:S(2)}) collective-permute-start(bf16[128,384]{0,1:T(8,128)(2,1)S(1)} %copy.89), channel_id=1, source_target_pairs={{0,8},{8,0},{16,24},{24,16},{32,40},{40,32},{48,56},{56,48},{64,72... | collective-permute-start | bytes 294920 | tf_op jit(solution)/shard_map/ppermute | solution.py:14
  10.8 4.8 %collective-permute-start = (bf16[128,384]{0,1:T(8,128)(2,1)S(1)}, bf16[128,384]{0,1:T(8,128)(2,1)S(1)}, u32[]{:S(2)}, u32[]{:S(2)}) collective-permute-start(bf16[128,384]{0,1:T(8,128)(2,1)S(1)} %copy.76), channel_id=1, source_target_pairs={{0,8},{8,0},{16,24},{24,16},{32,40},{40,32},{48,56},{56,48},{64,72... | collective-permute-start | bytes 294920 | tf_op jit(solution)/shard_map/ppermute | solution.py:14
  15.9 16.7 %collective-permute-start.4 = (bf16[256,384]{0,1:T(8,128)(2,1)S(1)}, bf16[256,384]{0,1:T(8,128)(2,1)S(1)}, u32[]{:S(2)}, u32[]{:S(2)}) collective-permute-start(bf16[256,384]{0,1:T(8,128)(2,1)S(1)} %pad_maximum_fusion.5), channel_id=1, source_target_pairs={{0,16},{8,24},{16,0},{24,8},{32,48},{40,56},{48,32},{56,40},{64,80... | collective-permute-start | bytes 589832 | tf_op jit(solution)/shard_map/ppermute | solution.py:14
  26.0 16.9 %collective-permute-start.1 = (bf16[256,384]{0,1:T(8,128)(2,1)S(1)}, bf16[256,384]{0,1:T(8,128)(2,1)S(1)}, u32[]{:S(2)}, u32[]{:S(2)}) collective-permute-start(bf16[256,384]{0,1:T(8,128)(2,1)S(1)} %pad_maximum_fusion.4), channel_id=1, source_target_pairs={{0,16},{8,24},{16,0},{24,8},{32,48},{40,56},{48,32},{56,40},{64,80... | collective-permute-start | bytes 589832 | tf_op jit(solution)/shard_map/ppermute | solution.py:14
  32.7 28.9 %collective-permute-start.5 = (bf16[512,384]{0,1:T(8,128)(2,1)S(1)}, bf16[512,384]{0,1:T(8,128)(2,1)S(1)}, u32[]{:S(2)}, u32[]{:S(2)}) collective-permute-start(bf16[512,384]{0,1:T(8,128)(2,1)S(1)} %pad_maximum_fusion.3), channel_id=1, source_target_pairs={{0,32},{8,40},{16,48},{24,56},{32,0},{40,8},{48,16},{56,24},{64,96... | collective-permute-start | bytes 1179656 | tf_op jit(solution)/shard_map/ppermute | solution.py:14
  42.9 17.9 %collective-permute-start.2 = (bf16[512,384]{0,1:T(8,128)(2,1)S(1)}, bf16[512,384]{0,1:T(8,128)(2,1)S(1)}, u32[]{:S(2)}, u32[]{:S(2)}) collective-permute-start(bf16[512,384]{0,1:T(8,128)(2,1)S(1)} %pad_maximum_fusion.2), channel_id=1, source_target_pairs={{0,32},{8,40},{16,48},{24,56},{32,0},{40,8},{48,16},{56,24},{64,96... | collective-permute-start | bytes 1179656 | tf_op jit(solution)/shard_map/ppermute | solution.py:14
  62.6 36.9 %collective-permute-start.7 = (bf16[1024,384]{0,1:T(8,128)(2,1)}, bf16[1024,384]{0,1:T(8,128)(2,1)S(1)}, u32[]{:S(2)}, u32[]{:S(2)}) collective-permute-start(bf16[1024,384]{0,1:T(8,128)(2,1)} %pad_maximum_fusion.1), channel_id=1, source_target_pairs={{0,64},{8,72},{16,80},{24,88},{32,96},{40,104},{48,112},{56,120},{... | collective-permute-start | bytes 2359304 | tf_op jit(solution)/shard_map/ppermute | solution.py:14
  68.3 31.2 %collective-permute-start.6 = (bf16[1024,384]{0,1:T(8,128)(2,1)}, bf16[1024,384]{0,1:T(8,128)(2,1)S(1)}, u32[]{:S(2)}, u32[]{:S(2)}) collective-permute-start(bf16[1024,384]{0,1:T(8,128)(2,1)} %pad_maximum_fusion), channel_id=1, source_target_pairs={{0,64},{8,72},{16,80},{24,88},{32,96},{40,104},{48,112},{56,120},{... | collective-permute-start | bytes 2359304 | tf_op jit(solution)/shard_map/ppermute | solution.py:14
  100.9 34.6 %collective-permute-start.9 = (bf16[2048,384]{0,1:T(8,128)(2,1)}, bf16[2048,384]{0,1:T(8,128)(2,1)}, u32[]{:S(2)}, u32[]{:S(2)}) collective-permute-start(bf16[2048,384]{0,1:T(8,128)(2,1)} %get-tuple-element.324), channel_id=1, source_target_pairs={{0,128},{8,136},{16,144},{24,152},{32,160},{40,168},{48,176},{56,1... | collective-permute-start | bytes 4718600 | tf_op jit(solution)/shard_map/ppermute | solution.py:14
  105.0 64.1 %collective-permute-start.8 = (bf16[2048,384]{0,1:T(8,128)(2,1)}, bf16[2048,384]{0,1:T(8,128)(2,1)}, u32[]{:S(2)}, u32[]{:S(2)}) collective-permute-start(bf16[2048,384]{0,1:T(8,128)(2,1)} %get-tuple-element.326), channel_id=1, source_target_pairs={{0,128},{8,136},{16,144},{24,152},{32,160},{40,168},{48,176},{56,1... | collective-permute-start | bytes 4718600 | tf_op jit(solution)/shard_map/ppermute | solution.py:14
  138.3 171.1 %collective-permute-start.11 = (bf16[4096,384]{0,1:T(8,128)(2,1)}, bf16[4096,384]{0,1:T(8,128)(2,1)}, u32[]{:S(2)}, u32[]{:S(2)}) collective-permute-start(bf16[4096,384]{0,1:T(8,128)(2,1)} %constant_dynamic-update-slice_fusion.16), channel_id=1, source_target_pairs={{0,256},{8,264},{16,272},{24,280},{32,288},{40,296},{48,304},{56,3... | collective-permute-start | bytes 9437192 | tf_op jit(solution)/shard_map/ppermute | solution.py:14
  173.5 132.0 %collective-permute-start.10 = (bf16[4096,384]{0,1:T(8,128)(2,1)}, bf16[4096,384]{0,1:T(8,128)(2,1)}, u32[]{:S(2)}, u32[]{:S(2)}) collective-permute-start(bf16[4096,384]{0,1:T(8,128)(2,1)} %constant_dynamic-update-slice_fusion.10), channel_id=1, source_target_pairs={{0,256},{8,264},{16,272},{24,280},{32,288},{40,296},{48,304},{56,3... | collective-permute-start | bytes 9437192 | tf_op jit(solution)/shard_map/ppermute | solution.py:14
where the time goes:
time: 380 us; the launch traced here: 375 us
  waiting for transfers between devices  210 us (55%)
  starting transfers between devices  57 us (15%)
  local copies, waits for them, and re-layouts  56.1 us (15%)
  blocking collectives  35 us (9%)
  matrix products  11.4 us (3%)
  other arithmetic  4.53 us (1%)
    ppermute x12, waiting for transfers between devices, from_partner(): return lax.ppermute(value, axis, pairs)  210 us
    ppermute x12, starting transfers between devices, from_partner(): return lax.ppermute(value, axis, pairs)  57 us
    all_to_all x1, blocking collectives, on_device(): lax.all_to_all(attended, 'ulysses', split_axis=0, concat_axis=1, tiled=True)  35 us
    dynamic_slice x42, local copies, waits for them, and re-layouts, fold_piece(): lax.scan(advance, running, (split_blocks(key_piece), split_blocks(value_p...  23.7 us
    unnamed x13, local copies, waits for them, and re-layouts  12.5 us
    ppermute x3, local copies, waits for them, and re-layouts, from_partner(): return lax.ppermute(value, axis, pairs)  7.64 us
  transfers between devices with their start and end apart: 12, of which 7 were waited for; matrix products, arithmetic and copies ran while one was open for 10% of the time, Pallas kernels for 0%

commit v1 on v0

v1 whole, which is shorter than its diff:
```python
import functools

import jax
import jax.numpy as jnp
from jax import lax
from jax.experimental import pallas as pl
from jax.experimental.pallas import tpu as pltpu
from jax.sharding import PartitionSpec as P

HD = 128
ROWS = 128
HALF = 64
OUT_ROWS = 16
MESH = pl.DeviceIdType.MESH
FACTOR = HD**-0.5 * 1.4426950408889634
F32 = jnp.float32
BF16 = jnp.bfloat16


def role(z):
    return 1 - lax.rem((z + 4) // 8, 2)


def soft_tile(keys_at, values_at, q, scores):
    peak = jnp.full((8, q.shape[0]), -jnp.inf, F32)
    for j in range(8):
        s = lax.dot_general(keys_at(j), q, (((1,), (1,)), ((), ())), preferred_element_type=F32)
        scores[j] = s
        peak = jnp.maximum(peak, jnp.max(s.reshape(32, 8, -1), axis=0))
    peak = jnp.max(peak, axis=0, keepdims=True)
    total = jnp.zeros((8, q.shape[0]), F32)
    sums = jnp.zeros((HD, q.shape[0]), F32)
    for j in range(8):
        p = jnp.exp2((scores[j] - peak) * FACTOR)
        total = total + jnp.sum(p.reshape(32, 8, -1), axis=0)
        sums = sums + jnp.dot(values_at(j), p.astype(BF16), preferred_element_type=F32)
    total = jnp.sum(total, axis=0, keepdims=True)
    return sums, peak, total


def pack(ref, at, sums, peak, total):
    ref[at, :HD] = sums
    ref[at, HD:] = jnp.concatenate([peak, total, jnp.zeros((6, peak.shape[1]), F32)], axis=0)


def merge(parts):
    peaks = [p[HD : HD + 1] for p in parts]
    top = functools.reduce(jnp.maximum, peaks)
    fades = [jnp.exp2((peak - top) * FACTOR) for peak in peaks]
    total = sum(p[HD + 1 : HD + 2] * f for p, f in zip(parts, fades))
    sums = sum(p[:HD] * f for p, f in zip(parts, fades))
    return (sums / total).T.astype(BF16)


def kernel(
    q_ref, k_ref, v_ref, o_ref,
    full, mid, full_q, mid_q, full_vt, mid_vt, scores,
    full_part, mid_part, full_got, mid_got, full_out, mid_out, landed,
    z_s, z_r, y_s, y_r, c_s, c_r, x_s, x_r, p_s, p_r, o_s, o_r,
):
    b = lax.axis_index("blk")
    zl = lax.axis_index("ulysses")
    c = lax.rem(b, 2)
    z = lax.rem(b // 2, 2) * 8 + zl
    y = lax.rem(b // 4, 4)
    x = b // 16

    def at(dx=0, dy=0, dz=0, dc=0):
        tx, ty = lax.rem(x + dx, 4), lax.rem(y + dy, 4)
        tz, tc = lax.rem(z + dz, 16), lax.rem(c + dc, 2)
        return (((tx * 4 + ty) * 2 + tz // 8) * 2 + tc, lax.rem(tz, 8))

    def copy(src, dst, s_sem, r_sem, where):
        return pltpu.make_async_remote_copy(
            src_ref=src, dst_ref=dst, send_sem=s_sem, recv_sem=r_sem, device_id=where, device_id_type=MESH
        )

    sent = []

    def send(*args):
        one = copy(*args)
        one.start()
        sent.append(one)

    barrier = pltpu.get_barrier_semaphore()
    peers = [at(dz=d) for d in range(1, 16)]
    peers += [at(dy=d) for d in range(1, 4)] + [at(dx=d) for d in range(1, 4)] + [at(dc=1)]
    for peer in peers:
        pl.semaphore_signal(barrier, inc=1, device_id=peer, device_id_type=MESH)
    pl.semaphore_wait(barrier, len(peers))

    mine = c * 4 + y
    here = at()
    holders = ((full, full_q, ROWS), (mid, mid_q, HALF))

    def z_dst(item, s):
        held, held_q, rows = holders[item // 3]
        if item % 3 == 0:
            return held_q.at[x, pl.ds(s * rows, rows)]
        return held.at[item % 3 - 1, mine, pl.ds(s * ROWS, ROWS)]

    for item in range(6):
        for s, dz in ((0, 4), (1, 12)):
            r = role(lax.rem(z + dz, 16))
            ref = (q_ref, k_ref, v_ref)[item % 3]
            if item < 3:
                src = ref.at[:, pl.ds(pl.multiple_of(r * 256, 128), HD)]
            elif item == 3:
                src = ref.at[pl.ds(pl.multiple_of(r * HALF, HALF), HALF), pl.ds(HD, HD)]
            else:
                src = ref.at[:, pl.ds(HD, HD)]
            send(src, z_dst(item, s), z_s.at[item, s], z_r.at[item, s], at(dz=dz))

    def z_wait(item, s):
        dst = z_dst(item, s)
        copy(dst, dst, z_s.at[item, s], z_r.at[item, s], here).wait_recv()

    def spread_queries(head):
        held_q, rows = holders[head][1:]
        for s in range(2):
            z_wait(head * 3, s)
            for dx in range(1, 4):
                part = held_q.at[x, pl.ds(s * rows, rows)]
                send(part, part, x_s.at[head, s, dx - 1], x_r.at[head, s, dx - 1], at(dx=dx))

    def wait_queries(head):
        held_q, rows = holders[head][1:]
        for s in range(2):
            for dx in range(1, 4):
                part = held_q.at[lax.rem(x - dx + 4, 4), pl.ds(s * rows, rows)]
                copy(part, part, x_s.at[head, s, dx - 1], x_r.at[head, s, dx - 1], here).wait_recv()

    def pass_on(head, kv, dy):
        held = holders[head][0]
        part = held.at[kv, c * 4 + lax.rem(y - dy + 4, 4)]
        send(part, part, c_s.at[head, kv, dy], c_r.at[head, kv, dy], at(dc=1))

    def spread_block(head, kv):
        held = holders[head][0]
        for s in range(2):
            z_wait(head * 3 + 1 + kv, s)
            for dy in range(1, 4):
                part = held.at[kv, mine, pl.ds(s * ROWS, ROWS)]
                send(part, part, y_s.at[head, kv, s, dy - 1], y_r.at[head, kv, s, dy - 1], at(dy=dy))
        pass_on(head, kv, 0)

    def relay_block(head, kv):
        held = holders[head][0]
        for dy in range(1, 4):
            for s in range(2):
                part = held.at[kv, c * 4 + lax.rem(y - dy + 4, 4), pl.ds(s * ROWS, ROWS)]
                copy(part, part, y_s.at[head, kv, s, dy - 1], y_r.at[head, kv, s, dy - 1], here).wait_recv()
            pass_on(head, kv, dy)

    def wait_block(head, kv):
        held = holders[head][0]
        for dy in range(4):
            part = held.at[kv, (1 - c) * 4 + lax.rem(y - dy + 4, 4)]
            copy(part, part, c_s.at[head, kv, dy], c_r.at[head, kv, dy], here).wait_recv()

    def turn_values(head, turned):
        held = holders[head][0]
        for j in range(8):
            turned[j] = held[1, j].T

    def send_part(head, dx):
        part, got = ((full_part, full_got), (mid_part, mid_got))[head]
        send(part.at[dx], got.at[dx - 1], p_s.at[head, dx - 1], p_r.at[head, dx - 1], at(dx=dx))

    def full_tile(dx):
        q = full_q[lax.rem(x + dx, 4)]
        pack(full_part, dx, *soft_tile(lambda j: full[0, j], lambda j: full_vt[j], q, scores))
        if dx:
            send_part(0, dx)

    def mid_tile(dx_a, dx_b):
        q = jnp.concatenate([mid_q[lax.rem(x + dx_a, 4)], mid_q[lax.rem(x + dx_b, 4)]], axis=0)
        sums, peak, total = soft_tile(lambda j: mid[0, j], lambda j: mid_vt[j], q, scores)
        for i, dx in enumerate((dx_a, dx_b)):
            cut = slice(i * ROWS, (i + 1) * ROWS)
            pack(mid_part, dx, sums[:, cut], peak[:, cut], total[:, cut])
            if dx:
                send_part(1, dx)

    def wait_parts(head):
        got = (full_got, mid_got)[head]
        for dx in range(1, 4):
            copy(got.at[dx - 1], got.at[dx - 1], p_s.at[head, dx - 1], p_r.at[head, dx - 1], here).wait_recv()

    spread_queries(0)
    spread_block(0, 0)
    spread_block(0, 1)
    relay_block(0, 0)
    spread_queries(1)
    relay_block(0, 1)
    wait_queries(0)
    wait_block(0, 0)
    wait_block(0, 1)
    turn_values(0, full_vt)
    full_tile(2)
    spread_block(1, 0)
    full_tile(1)
    full_tile(3)
    spread_block(1, 1)
    full_tile(0)
    relay_block(1, 0)
    relay_block(1, 1)
    wait_queries(1)
    wait_block(1, 0)
    wait_block(1, 1)
    turn_values(1, mid_vt)
    mid_tile(2, 1)
    mid_tile(3, 0)

    r = role(z)
    first = lax.rem(z + 12, 16) // 8
    head_base = lax.rem(z + 4, 8) * 3

    def hand_over(out, row, head, tz, sem):
        src = out.at[pl.ds(pl.multiple_of(row, OUT_ROWS), OUT_ROWS)]
        dst = landed.at[:, pl.ds(pl.multiple_of(head * HD, HD), HD)]
        return src, dst, sem, o_r, (((x * 4 + y) * 2 + tz // 8) * 2 + c, lax.rem(tz, 8))

    wait_parts(0)
    full_out[...] = merge([full_part[0]] + [full_got[i] for i in range(3)])
    for d in range(16):
        tz = lax.rem(z + d, 16)
        s = lax.rem(first + tz // 8, 2)
        move = hand_over(full_out, s * ROWS + lax.rem(tz, 8) * OUT_ROWS, head_base + 2 * r, tz, o_s.at[d])
        if d:
            send(*move)
        else:
            pltpu.make_async_copy(move[0], move[1], o_r).start()

    wait_parts(1)
    mid_out[...] = merge([mid_part[0]] + [mid_got[i] for i in range(3)])
    late = []
    for half in range(2):
        for i in range(4):
            tz = half * 8 + 4 * r + i
            s = lax.rem(first + half, 2)
            move = hand_over(mid_out, s * HALF + i * OUT_ROWS, head_base + 1, tz, o_s.at[16 + half * 4 + i])
            one = copy(*move)
            late.append((tz, one))

            @pl.when(tz != z)
            def _():
                one.start()

            @pl.when(tz == z)
            def _():
                pltpu.make_async_copy(move[0], move[1], o_r).start()

    pltpu.make_async_copy(landed, landed, o_r).wait()
    o_ref[...] = landed[...]
    for one in sent:
        one.wait_send()
    for tz, one in late:

        @pl.when(tz != z)
        def _():
            one.wait_send()


def on_device(query_rows, key_rows, value_rows):
    dma = pltpu.SemaphoreType.DMA
    return pl.pallas_call(
        kernel,
        out_shape=jax.ShapeDtypeStruct((OUT_ROWS, 24 * HD), BF16),
        in_specs=[pl.BlockSpec(memory_space=pl.ANY)] * 3,
        out_specs=pl.BlockSpec(memory_space=pltpu.VMEM),
        scratch_shapes=[
            pltpu.VMEM((2, 8, 256, HD), BF16),
            pltpu.VMEM((2, 8, 256, HD), BF16),
            pltpu.VMEM((4, 256, HD), BF16),
            pltpu.VMEM((4, 128, HD), BF16),
            pltpu.VMEM((8, HD, 256), BF16),
            pltpu.VMEM((8, HD, 256), BF16),
            pltpu.VMEM((8, 256, 256), F32),
            pltpu.VMEM((4, HD + 8, 256), F32),
            pltpu.VMEM((4, HD + 8, 128), F32),
            pltpu.VMEM((3, HD + 8, 256), F32),
            pltpu.VMEM((3, HD + 8, 128), F32),
            pltpu.VMEM((256, HD), BF16),
            pltpu.VMEM((128, HD), BF16),
            pltpu.VMEM((OUT_ROWS, 24 * HD), BF16),
            dma((6, 2)), dma((6, 2)),
            dma((2, 2, 2, 3)), dma((2, 2, 2, 3)),
            dma((2, 2, 4)), dma((2, 2, 4)),
            dma((2, 2, 3)), dma((2, 2, 3)),
            dma((2, 3)), dma((2, 3)),
            dma((24,)), dma(()),
        ],
        compiler_params=pltpu.CompilerParams(
            collective_id=0, has_side_effects=True, vmem_limit_bytes=40 * 2**20
        ),
        name="attend",
    )(query_rows, key_rows, value_rows)


def solution(mesh):
    return jax.shard_map(
        on_device,
        mesh=mesh,
        in_specs=(P("blk", "ulysses"), P("blk", "ulysses"), P("blk", "ulysses")),
        out_specs=P(("blk", "ulysses"), None),
        check_vma=False,
    )
```

time: 380 us -> 67.5 us (0.18); the launches traced: 375 us -> 67.3 us
  waiting for transfers between devices: 210 us -> 0 us
  Pallas kernels: 0 us -> 63.9 us
  starting transfers between devices: 57 us -> 0 us
  local copies, waits for them, and re-layouts: 56.1 us -> 3.32 us
  blocking collectives: 35 us -> 0 us
  matrix products: 11.4 us -> 0 us
  other arithmetic: 4.53 us -> 0 us
    ppermute x12 -> x0, waiting for transfers between devices: 210 us -> none  [from_partner(): return lax.ppermute(value, axis, pairs)]
    pallas_call x0 -> x1, Pallas kernels: none -> 63.9 us  [on_device(): pl.pallas_call(kernel, out_shape=jax.ShapeDtypeStruct((OUT_ROWS, 24 * HD)...]
    ppermute x12 -> x0, starting transfers between devices: 57 us -> none  [from_partner(): return lax.ppermute(value, axis, pairs)]
    all_to_all x1 -> x0, blocking collectives: 35 us -> none  [on_device(): lax.all_to_all(attended, 'ulysses', split_axis=0, concat_axis=1, tiled=True)]
    dynamic_slice x42 -> x0, local copies, waits for them, and re-layouts: 23.7 us -> none  [fold_piece(): lax.scan(advance, running, (split_blocks(key_piece), split_blocks(value_p...]
    dot_general x36 -> x0, matrix products: 11.4 us -> none  [the longest x18 5.75 us: block_scores(): jnp.einsum('rhd,khd->rhk', query_heads, key_heads, preferred_element_type...]
    unnamed x13 -> x7, local copies, waits for them, and re-layouts: 12.5 us -> 3.32 us
    ppermute x3 -> x0, local copies, waits for them, and re-layouts: 7.64 us -> none  [from_partner(): return lax.ppermute(value, axis, pairs)]
  transfers between devices with their start and end apart: 12 -> 0, of which waited for: 7 -> 0; matrix products, arithmetic and copies ran while one was open for 10% -> 0% of each run, Pallas kernels for 0% -> 0%
where the time goes in v1:
time: 67.5 us; the launch traced here: 67.3 us
  Pallas kernels  63.9 us (95%)
  local copies, waits for them, and re-layouts  3.32 us (5%)
    pallas_call x1, Pallas kernels, on_device(): pl.pallas_call(kernel, out_shape=jax.ShapeDtypeStruct((OUT_ROWS, 24 * HD)...  63.9 us
    unnamed x7, local copies, waits for them, and re-layouts  3.32 us

profile of v1, /device:TPU:1, one launch (start us, length us, event | category | flops | bytes accessed | tf_op | source)
XLA Modules:
  0.0 67.3 jit_solution(4401283076180158048)
XLA Ops:
  0.0 0.0 copy-start
  0.0 0.9 %copy-done = bf16[128,384]{1,0:T(8,128)(2,1)S(1)} copy-done((bf16[128,384]{1,0:T(8,128)(2,1)S(1)}, bf16[128,384]{1,0:T(8,128)(2,1)}, u32[]{:S(2)}) %copy-start) | copy-done | bytes 98328
  0.9 0.0 copy-start.1
  0.9 0.9 %copy-done.1 = bf16[128,384]{1,0:T(8,128)(2,1)S(1)} copy-done((bf16[128,384]{1,0:T(8,128)(2,1)S(1)}, bf16[128,384]{1,0:T(8,128)(2,1)}, u32[]{:S(2)}) %copy-start.1) | copy-done | bytes 98328
  1.8 0.0 copy-start.2
  1.8 0.9 %copy-done.2 = bf16[128,384]{1,0:T(8,128)(2,1)S(1)} copy-done((bf16[128,384]{1,0:T(8,128)(2,1)S(1)}, bf16[128,384]{1,0:T(8,128)(2,1)}, u32[]{:S(2)}) %copy-start.2) | copy-done | bytes 98328
  2.7 63.9 %attend.1 = bf16[16,3072]{1,0:T(8,128)(2,1)S(1)} custom-call(bf16[128,384]{1,0:T(8,128)(2,1)S(1)} %copy-done, bf16[128,384]{1,0:T(8,128)(2,1)S(1)} %copy-done.1, bf16[128,384]{1,0:T(8,128)(2,1)S(1)} %copy-done.2), custom_call_target="tpu_custom_call" | custom-call | tf_op jit(solution)/shard_map/attend/pallas_call | solution.py:267
  66.6 0.6 copy.5
Async XLA Ops:
  0.0 0.9 %copy-start = (bf16[128,384]{1,0:T(8,128)(2,1)S(1)}, bf16[128,384]{1,0:T(8,128)(2,1)}, u32[]{:S(2)}) copy-start(bf16[128,384]{1,0:T(8,128)(2,1)} %q_ref.1) | copy-start | bytes 294916
  0.9 0.9 %copy-start.1 = (bf16[128,384]{1,0:T(8,128)(2,1)S(1)}, bf16[128,384]{1,0:T(8,128)(2,1)}, u32[]{:S(2)}) copy-start(bf16[128,384]{1,0:T(8,128)(2,1)} %k_ref.1) | copy-start | bytes 294916
  1.8 0.9 %copy-start.2 = (bf16[128,384]{1,0:T(8,128)(2,1)S(1)}, bf16[128,384]{1,0:T(8,128)(2,1)}, u32[]{:S(2)}) copy-start(bf16[128,384]{1,0:T(8,128)(2,1)} %v_ref.1) | copy-start | bytes 294916

commit v2 on v1

v2 whole, which is shorter than its diff:
```python
import functools

import jax
import jax.numpy as jnp
from jax import lax
from jax.experimental import pallas as pl
from jax.experimental.pallas import tpu as pltpu
from jax.sharding import PartitionSpec as P

HD = 128
ROWS = 128
HALF = 64
OUT_ROWS = 16
MESH = pl.DeviceIdType.MESH
FACTOR = HD**-0.5 * 1.4426950408889634
F32 = jnp.float32
BF16 = jnp.bfloat16


def role(z):
    return 1 - lax.rem((z + 4) // 8, 2)


def weigh_tile(keys_at, q, scores, weights):
    peak = jnp.full((8, q.shape[0]), -jnp.inf, F32)
    for j in range(8):
        s = lax.dot_general(keys_at(j), q, (((1,), (1,)), ((), ())), preferred_element_type=F32)
        scores[j] = s
        peak = jnp.maximum(peak, jnp.max(s.reshape(32, 8, -1), axis=0))
    peak = jnp.max(peak, axis=0, keepdims=True)
    total = jnp.zeros((8, q.shape[0]), F32)
    for j in range(8):
        p = jnp.exp2((scores[j] - peak) * FACTOR)
        total = total + jnp.sum(p.reshape(32, 8, -1), axis=0)
        weights[j] = p.astype(BF16)
    return peak, jnp.sum(total, axis=0, keepdims=True)


def sum_tile(values_at, weights):
    return sum(jnp.dot(values_at(j), weights[j], preferred_element_type=F32) for j in range(8))


def pack(ref, at, sums, peak, total):
    ref[at, :HD] = sums
    ref[at, HD:] = jnp.concatenate([peak, total, jnp.zeros((6, peak.shape[1]), F32)], axis=0)


def merge(parts):
    peaks = [p[HD : HD + 1] for p in parts]
    top = functools.reduce(jnp.maximum, peaks)
    fades = [jnp.exp2((peak - top) * FACTOR) for peak in peaks]
    total = sum(p[HD + 1 : HD + 2] * f for p, f in zip(parts, fades))
    sums = sum(p[:HD] * f for p, f in zip(parts, fades))
    return (sums / total).T.astype(BF16)


def kernel(
    q_ref, k_ref, v_ref, o_ref,
    full, mid, full_q, mid_q, full_vt, mid_vt, scores, weights,
    full_part, mid_part, full_got, mid_got, full_out, mid_out, landed,
    z_s, z_r, y_s, y_r, c_s, c_r, x_s, x_r, p_s, p_r, o_s, o_r,
):
    b = lax.axis_index("blk")
    zl = lax.axis_index("ulysses")
    c = lax.rem(b, 2)
    z = lax.rem(b // 2, 2) * 8 + zl
    y = lax.rem(b // 4, 4)
    x = b // 16

    def at(dx=0, dy=0, dz=0, dc=0):
        tx, ty = lax.rem(x + dx, 4), lax.rem(y + dy, 4)
        tz, tc = lax.rem(z + dz, 16), lax.rem(c + dc, 2)
        return (((tx * 4 + ty) * 2 + tz // 8) * 2 + tc, lax.rem(tz, 8))

    def copy(src, dst, s_sem, r_sem, where):
        return pltpu.make_async_remote_copy(
            src_ref=src, dst_ref=dst, send_sem=s_sem, recv_sem=r_sem, device_id=where, device_id_type=MESH
        )

    def send(*args):
        copy(*args).start()

    def landed_all(ref, sem):
        pltpu.make_async_copy(ref, ref, sem).wait()

    barrier = pltpu.get_barrier_semaphore()
    peers = [at(dz=d) for d in (1, 2, 4, 12, 14, 15)]
    peers += [at(dy=d) for d in range(1, 4)] + [at(dx=d) for d in range(1, 4)] + [at(dc=1)]
    for peer in peers:
        pl.semaphore_signal(barrier, inc=1, device_id=peer, device_id_type=MESH)
    pl.semaphore_wait(barrier, len(peers))

    holders = ((full, full_q, ROWS), (mid, mid_q, HALF))
    block_at, query_at = (y, y), (x, x)

    def along_blocks(head, d):
        return at(dy=d)

    def along_queries(head, d):
        return at(dx=d)

    def block_from(head, d):
        return c * 4 + lax.rem(block_at[head] - d + 4, 4)

    def z_start(head, item):
        held, held_q, rows = holders[head]
        for s, dz in ((0, 4), (1, 12)):
            r = role(lax.rem(z + dz, 16))
            ref = (k_ref, v_ref, q_ref)[item]
            if head == 0:
                src = ref.at[:, pl.ds(pl.multiple_of(r * 256, 128), HD)]
            elif item == 2:
                src = ref.at[pl.ds(pl.multiple_of(r * HALF, HALF), HALF), pl.ds(HD, HD)]
            else:
                src = ref.at[:, pl.ds(HD, HD)]
            if item == 2:
                dst = held_q.at[query_at[head], pl.ds(s * rows, rows)]
            else:
                dst = held.at[item, block_from(head, 0), pl.ds(s * ROWS, ROWS)]
            send(src, dst, z_s.at[head, item], z_r.at[head, item], at(dz=dz))

    def z_sent(head, item):
        held, held_q, rows = holders[head]
        landed_all(held_q.at[0] if item == 2 else held.at[item, 0], z_s.at[head, item])

    def z_wait(head, item):
        held, held_q, rows = holders[head]
        landed_all(held_q.at[query_at[head]] if item == 2 else held.at[item, block_from(head, 0)], z_r.at[head, item])

    def spread_queries(head):
        held_q = holders[head][1]
        z_wait(head, 2)
        part = held_q.at[query_at[head]]
        for d in range(1, 4):
            send(part, part, x_s, x_r.at[head], along_queries(head, d))

    def wait_queries(head):
        held_q = holders[head][1]
        landed_all(held_q.at[pl.ds(0, 3)], x_r.at[head])

    def pass_on(head, kv, d):
        part = holders[head][0].at[kv, block_from(head, d)]
        send(part, part, c_s, c_r.at[head, kv], at(dc=1))

    def spread_block(head, kv):
        part = holders[head][0].at[kv, block_from(head, 0)]
        z_wait(head, kv)
        for d in range(1, 4):
            send(part, part, y_s, y_r.at[head, kv, d - 1], along_blocks(head, d))
        pass_on(head, kv, 0)

    def relay_block(head, kv):
        for d in range(1, 4):
            landed_all(holders[head][0].at[kv, block_from(head, d)], y_r.at[head, kv, d - 1])
            pass_on(head, kv, d)

    def wait_block(head, kv):
        landed_all(holders[head][0].at[kv, pl.ds((1 - c) * 4, 4)], c_r.at[head, kv])

    def turn_values(head, turned):
        held = holders[head][0]
        for j in range(8):
            turned[j] = held[1, j].T

    def send_part(head, d):
        part, got = ((full_part, full_got), (mid_part, mid_got))[head]
        send(part.at[d], got.at[d - 1], p_s.at[head], p_r.at[head], along_queries(head, d))

    def full_tile(d):
        q = full_q[lax.rem(query_at[0] + d, 4)]
        peak, total = weigh_tile(lambda j: full[0, j], q, scores, weights.at[0])
        pack(full_part, d, sum_tile(lambda j: full_vt[j], weights.at[0]), peak, total)
        if d:
            send_part(0, d)

    def mid_weigh(i, d_a, d_b):
        q = jnp.concatenate([mid_q[lax.rem(query_at[1] + d, 4)] for d in (d_a, d_b)], axis=0)
        return weigh_tile(lambda j: mid[0, j], q, scores, weights.at[i])

    def mid_sum(i, d_a, d_b, peak, total):
        sums = sum_tile(lambda j: mid_vt[j], weights.at[i])
        for k, d in enumerate((d_a, d_b)):
            cut = slice(k * ROWS, (k + 1) * ROWS)
            pack(mid_part, d, sums[:, cut], peak[:, cut], total[:, cut])
            if d:
                send_part(1, d)

    z_start(0, 0)
    z_start(0, 1)
    z_sent(0, 0)
    z_sent(0, 1)
    z_start(1, 0)
    z_start(0, 2)
    spread_block(0, 0)
    spread_block(0, 1)
    z_sent(1, 0)
    z_sent(0, 2)
    z_start(1, 1)
    z_start(1, 2)
    relay_block(0, 0)
    spread_block(1, 0)
    spread_queries(0)
    relay_block(0, 1)
    spread_block(1, 1)
    spread_queries(1)
    relay_block(1, 0)
    wait_block(0, 0)
    wait_block(0, 1)
    turn_values(0, full_vt)
    wait_queries(0)
    full_tile(2)
    full_tile(1)
    relay_block(1, 1)
    full_tile(3)
    full_tile(0)
    wait_block(1, 0)
    wait_queries(1)
    first_pair = mid_weigh(0, 2, 1)
    other_pair = mid_weigh(1, 3, 0)
    wait_block(1, 1)
    turn_values(1, mid_vt)
    mid_sum(0, 2, 1, *first_pair)
    mid_sum(1, 3, 0, *other_pair)
    z_sent(1, 1)
    z_sent(1, 2)

    r = role(z)
    first = lax.rem(z + 12, 16) // 8
    head_base = lax.rem(z + 4, 8) * 3

    def hand_over(out, row, head, tz, sem):
        src = out.at[pl.ds(pl.multiple_of(row, OUT_ROWS), OUT_ROWS)]
        dst = landed.at[:, pl.ds(pl.multiple_of(head * HD, HD), HD)]
        return src, dst, sem, o_r, (((x * 4 + y) * 2 + tz // 8) * 2 + c, lax.rem(tz, 8))

    landed_all(full_got, p_r.at[0])
    full_out[...] = merge([full_part[0]] + [full_got[i] for i in range(3)])
    for d in range(16):
        tz = lax.rem(z + d, 16)
        s = lax.rem(first + tz // 8, 2)
        move = hand_over(full_out, s * ROWS + lax.rem(tz, 8) * OUT_ROWS, head_base + 2 * r, tz, o_s.at[0])
        if d:
            send(*move)
        else:
            pltpu.make_async_copy(move[0], move[1], o_r).start()

    landed_all(mid_got, p_r.at[1])
    mid_out[...] = merge([mid_part[0]] + [mid_got[i] for i in range(3)])
    for half in range(2):
        for i in range(4):
            tz = half * 8 + 4 * r + i
            s = lax.rem(first + half, 2)
            move = hand_over(mid_out, s * HALF + i * OUT_ROWS, head_base + 1, tz, o_s.at[1])

            @pl.when(tz != z)
            def _():
                send(*move)

            @pl.when(tz == z)
            def _():
                pltpu.make_async_copy(move[0], move[1], o_r).start()

    landed_all(landed, o_r)
    o_ref[...] = landed[...]
    landed_all(full.at[:, pl.ds(0, 6)], y_s)
    landed_all(full, c_s)
    landed_all(full.at[0, :, pl.ds(0, 144)], x_s)
    landed_all(full_got, p_s.at[0])
    landed_all(mid_got, p_s.at[1])
    landed_all(landed.at[:, pl.ds(0, 15 * HD)], o_s.at[0])

    @pl.when(z < 8)
    def _():
        landed_all(landed.at[:, pl.ds(0, 8 * HD)], o_s.at[1])

    @pl.when(z >= 8)
    def _():
        landed_all(landed.at[:, pl.ds(0, 7 * HD)], o_s.at[1])


def on_device(query_rows, key_rows, value_rows):
    dma = pltpu.SemaphoreType.DMA
    return pl.pallas_call(
        kernel,
        out_shape=jax.ShapeDtypeStruct((OUT_ROWS, 24 * HD), BF16),
        in_specs=[pl.BlockSpec(memory_space=pl.ANY)] * 3,
        out_specs=pl.BlockSpec(memory_space=pltpu.VMEM),
        scratch_shapes=[
            pltpu.VMEM((2, 8, 256, HD), BF16),
            pltpu.VMEM((2, 8, 256, HD), BF16),
            pltpu.VMEM((4, 256, HD), BF16),
            pltpu.VMEM((4, 128, HD), BF16),
            pltpu.VMEM((8, HD, 256), BF16),
            pltpu.VMEM((8, HD, 256), BF16),
            pltpu.VMEM((8, 256, 256), F32),
            pltpu.VMEM((2, 8, 256, 256), BF16),
            pltpu.VMEM((4, HD + 8, 256), F32),
            pltpu.VMEM((4, HD + 8, 128), F32),
            pltpu.VMEM((3, HD + 8, 256), F32),
            pltpu.VMEM((3, HD + 8, 128), F32),
            pltpu.VMEM((256, HD), BF16),
            pltpu.VMEM((128, HD), BF16),
            pltpu.VMEM((OUT_ROWS, 24 * HD), BF16),
            dma((2, 3)), dma((2, 3)),
            dma(()), dma((2, 2, 3)),
            dma(()), dma((2, 2)),
            dma(()), dma((2,)),
            dma((2,)), dma((2,)),
            dma((2,)), dma(()),
        ],
        compiler_params=pltpu.CompilerParams(
            collective_id=0, has_side_effects=True, vmem_limit_bytes=60 * 2**20
        ),
        name="attend",
    )(query_rows, key_rows, value_rows)


def solution(mesh):
    return jax.shard_map(
        on_device,
        mesh=mesh,
        in_specs=(P("blk", "ulysses"), P("blk", "ulysses"), P("blk", "ulysses")),
        out_specs=P(("blk", "ulysses"), None),
        check_vma=False,
    )
```

time: 67.5 us -> 57.7 us (0.85)
  the two profiles are of different devices: /device:TPU:1 before, /device:TPU:2 now
where the time goes in v2:
time: 57.7 us; the launch traced here: 57.5 us
  Pallas kernels  56 us (97%)
  local copies, waits for them, and re-layouts  1.54 us (3%)
    pallas_call x1, Pallas kernels, on_device(): pl.pallas_call(kernel, out_shape=jax.ShapeDtypeStruct((OUT_ROWS, 24 * HD)...  56 us
    unnamed x1, local copies, waits for them, and re-layouts  1.54 us

profile of v2, /device:TPU:2, one launch (start us, length us, event | category | flops | bytes accessed | tf_op | source)
XLA Modules:
  0.0 57.5 jit_solution(6778437536309049121)
XLA Ops:
  0.0 56.0 %attend.1 = bf16[16,3072]{1,0:T(8,128)(2,1)} custom-call(bf16[128,384]{1,0:T(8,128)(2,1)} %q_ref.1, bf16[128,384]{1,0:T(8,128)(2,1)} %k_ref.1, bf16[128,384]{1,0:T(8,128)(2,1)} %v_ref.1), custom_call_target="tpu_custom_call" | custom-call | tf_op jit(solution)/shard_map/attend/pallas_call | solution.py:283
  56.0 1.5 %copy.5 = bf16[16,3072]{1,0:T(8,128)(2,1)} copy(bf16[16,3072]{1,0:T(8,128)(2,1)} %attend.1) | data formatting | bytes 196608

commit v3 on v2

v3 whole, which is shorter than its diff:
```python
import functools

import jax
import jax.numpy as jnp
from jax import lax
from jax.experimental import pallas as pl
from jax.experimental.pallas import tpu as pltpu
from jax.sharding import PartitionSpec as P

HD = 128
ROWS = 128
OUT_ROWS = 16
MESH = pl.DeviceIdType.MESH
FACTOR = HD**-0.5 * 1.4426950408889634
F32 = jnp.float32
BF16 = jnp.bfloat16


def role(z):
    return 1 - lax.rem((z + 4) // 8, 2)


def weigh_tile(keys_at, q, scores, weights):
    peak = jnp.full((8, q.shape[0]), -jnp.inf, F32)
    for j in range(8):
        s = lax.dot_general(keys_at(j), q, (((1,), (1,)), ((), ())), preferred_element_type=F32)
        scores[j] = s
        peak = jnp.maximum(peak, jnp.max(s.reshape(32, 8, -1), axis=0))
    peak = jnp.max(peak, axis=0, keepdims=True)
    total = jnp.zeros((8, q.shape[0]), F32)
    for j in range(8):
        p = jnp.exp2((scores[j] - peak) * FACTOR)
        total = total + jnp.sum(p.reshape(32, 8, -1), axis=0)
        weights[j] = p.astype(BF16)
    return peak, jnp.sum(total, axis=0, keepdims=True)


def sum_tile(values_at, weights):
    return sum(jnp.dot(values_at(j), weights[j], preferred_element_type=F32) for j in range(8))


def pack(ref, at, sums, peak, total):
    ref[at, :HD] = sums
    ref[at, HD:] = jnp.concatenate([peak, total, jnp.zeros((6, peak.shape[1]), F32)], axis=0)


def merge(parts):
    peaks = [p[HD : HD + 1] for p in parts]
    top = functools.reduce(jnp.maximum, peaks)
    fades = [jnp.exp2((peak - top) * FACTOR) for peak in peaks]
    total = sum(p[HD + 1 : HD + 2] * f for p, f in zip(parts, fades))
    sums = sum(p[:HD] * f for p, f in zip(parts, fades))
    return (sums / total).T.astype(BF16)


def kernel(
    q_ref, k_ref, v_ref, o_ref,
    full, mid, full_q, mid_q, full_vt, mid_vt, scores, weights,
    full_part, mid_part, full_got, mid_got, full_out, mid_out, landed,
    z_s, z_r, y_s, y_r, c_s, c_r, x_s, x_r, p_s, p_r, o_s, o_r, l_s,
):
    b = lax.axis_index("blk")
    zl = lax.axis_index("ulysses")
    c = lax.rem(b, 2)
    z = lax.rem(b // 2, 2) * 8 + zl
    y = lax.rem(b // 4, 4)
    x = b // 16

    def at(dx=0, dy=0, dz=0, dc=0):
        tx, ty = lax.rem(x + dx, 4), lax.rem(y + dy, 4)
        tz, tc = lax.rem(z + dz, 16), lax.rem(c + dc, 2)
        return (((tx * 4 + ty) * 2 + tz // 8) * 2 + tc, lax.rem(tz, 8))

    def copy(src, dst, s_sem, r_sem, where):
        return pltpu.make_async_remote_copy(
            src_ref=src, dst_ref=dst, send_sem=s_sem, recv_sem=r_sem, device_id=where, device_id_type=MESH
        )

    def send(*args):
        copy(*args).start()

    def landed_all(ref, sem):
        pltpu.make_async_copy(ref, ref, sem).wait()

    barrier = pltpu.get_barrier_semaphore()
    peers = [at(dz=d) for d in (1, 2, 4, 12, 14, 15)]
    peers += [at(dy=d) for d in range(1, 4)] + [at(dx=d) for d in range(1, 4)] + [at(dc=1)]
    for peer in peers:
        pl.semaphore_signal(barrier, inc=1, device_id=peer, device_id_type=MESH)
    pl.semaphore_wait(barrier, len(peers))

    held_by, queries_by = (full, mid), (full_q, mid_q)
    columns = pl.ds(HD, HD)

    def block(head, kv, d, s=None):
        ref = held_by[head].at[kv, c * 4 + lax.rem(y - d + 4, 4)]
        return ref if s is None else ref.at[pl.ds(s * ROWS, ROWS)]

    def z_start(item):
        for s, dz in ((0, 4), (1, 12)):
            r = role(lax.rem(z + dz, 16))
            src = (k_ref, v_ref, q_ref)[item].at[:, pl.ds(pl.multiple_of(r * 256, 128), HD)]
            dst = full_q.at[x, pl.ds(s * ROWS, ROWS)] if item == 2 else block(0, item, 0, s)
            send(src, dst, z_s.at[item], z_r.at[item], at(dz=dz))

    def z_ref(item):
        return full_q.at[x] if item == 2 else block(0, item, 0)

    def z_sent(item):
        landed_all(z_ref(item), z_s.at[item])

    def m_start(kv):
        src = (k_ref, v_ref)[kv].at[:, columns]
        send(src, block(1, kv, 0, 1), z_s.at[3 + kv], z_r.at[3 + kv], at(dz=8))

    def m_sent(kv):
        landed_all(block(1, kv, 0, 1), z_s.at[3 + kv])

    def own_queries():
        src, dst = q_ref.at[:, columns], mid_q.at[x]
        for d in range(1, 4):
            send(src, dst, x_s, x_r.at[1], at(dx=d))
        pltpu.make_async_copy(src, dst, l_s).start()

    def own_block(kv):
        src, dst = (k_ref, v_ref)[kv].at[:, columns], block(1, kv, 0, 0)
        for d in range(1, 4):
            send(src, dst, y_s, y_r.at[2 + kv, d - 1], at(dy=d))
        send(src, dst, c_s, c_r.at[2 + kv], at(dc=1))
        pltpu.make_async_copy(src, dst, l_s).start()

    def own_landed():
        landed_all(mid.at[0, pl.ds(0, 3), pl.ds(0, ROWS)], l_s)

    def spread_queries():
        landed_all(z_ref(2), z_r.at[2])
        for d in range(1, 4):
            send(full_q.at[x], full_q.at[x], x_s, x_r.at[0], at(dx=d))

    def wait_queries(head):
        landed_all(queries_by[head].at[pl.ds(0, 3)], x_r.at[head])

    def kind_block(kind, d):
        return block(0, kind, d) if kind < 2 else block(1, kind % 2, d, kind // 2 - 1)

    def pass_on(kind, d):
        part = kind_block(kind, d)
        send(part, part, c_s, c_r.at[kind], at(dc=1))

    def spread_block(kind):
        part = kind_block(kind, 0)
        landed_all(part, z_r.at[kind if kind < 2 else kind - 1])
        for d in range(1, 4):
            send(part, part, y_s, y_r.at[kind, d - 1], at(dy=d))
        pass_on(kind, 0)

    def relay_block(kind):
        for d in range(1, 4):
            landed_all(kind_block(kind, d), y_r.at[kind, d - 1])
            pass_on(kind, d)

    def wait_block(kind):
        other = pl.ds((1 - c) * 4, 4)
        if kind < 2:
            landed_all(full.at[kind, other], c_r.at[kind])
        else:
            landed_all(mid.at[kind % 2, other, pl.ds((kind // 2 - 1) * ROWS, ROWS)], c_r.at[kind])

    def turn_values(head, turned):
        for j in range(8):
            turned[j] = held_by[head][1, j].T

    def send_part(head, d):
        part, got = ((full_part, full_got), (mid_part, mid_got))[head]
        send(part.at[d], got.at[d - 1], p_s.at[head], p_r.at[head], at(dx=d))

    def full_tile(d):
        q = full_q[lax.rem(x + d, 4)]
        peak, total = weigh_tile(lambda j: full[0, j], q, scores, weights.at[0])
        pack(full_part, d, sum_tile(lambda j: full_vt[j], weights.at[0]), peak, total)
        if d:
            send_part(0, d)

    def mid_weigh(i, d_a, d_b):
        q = jnp.concatenate([mid_q[lax.rem(x + d, 4)] for d in (d_a, d_b)], axis=0)
        return weigh_tile(lambda j: mid[0, j], q, scores, weights.at[i])

    def mid_sum(i, d_a, d_b, peak, total):
        sums = sum_tile(lambda j: mid_vt[j], weights.at[i])
        for k, d in enumerate((d_a, d_b)):
            cut = slice(k * ROWS, (k + 1) * ROWS)
            pack(mid_part, d, sums[:, cut], peak[:, cut], total[:, cut])
            if d:
                send_part(1, d)

    z_start(0)
    z_start(1)
    z_start(2)
    own_queries()
    own_block(0)
    own_block(1)
    relay_block(2)
    relay_block(3)
    spread_block(0)
    m_start(0)
    m_start(1)
    spread_block(1)
    spread_queries()
    relay_block(0)
    relay_block(1)
    wait_block(0)
    wait_block(1)
    turn_values(0, full_vt)
    wait_queries(0)
    full_tile(2)
    spread_block(4)
    full_tile(1)
    spread_block(5)
    full_tile(3)
    full_tile(0)
    relay_block(4)
    relay_block(5)
    own_landed()
    wait_queries(1)
    wait_block(2)
    wait_block(3)
    wait_block(4)
    first_pair = mid_weigh(0, 2, 1)
    other_pair = mid_weigh(1, 3, 0)
    wait_block(5)
    turn_values(1, mid_vt)
    mid_sum(0, 2, 1, *first_pair)
    mid_sum(1, 3, 0, *other_pair)
    z_sent(0)
    z_sent(1)
    z_sent(2)
    m_sent(0)
    m_sent(1)

    r = role(z)
    first = lax.rem(z + 12, 16) // 8
    head_base = lax.rem(z + 4, 8) * 3

    def hand_over(out, row, head, tz, sem):
        src = out.at[pl.ds(pl.multiple_of(row, OUT_ROWS), OUT_ROWS)]
        dst = landed.at[:, pl.ds(pl.multiple_of(head * HD, HD), HD)]
        return src, dst, sem, o_r, (((x * 4 + y) * 2 + tz // 8) * 2 + c, lax.rem(tz, 8))

    landed_all(full_got, p_r.at[0])
    full_out[...] = merge([full_part[0]] + [full_got[i] for i in range(3)])
    for d in range(16):
        tz = lax.rem(z + d, 16)
        s = lax.rem(first + tz // 8, 2)
        move = hand_over(full_out, s * ROWS + lax.rem(tz, 8) * OUT_ROWS, head_base + 2 * r, tz, o_s.at[0])
        if d:
            send(*move)
        else:
            pltpu.make_async_copy(move[0], move[1], o_r).start()

    landed_all(mid_got, p_r.at[1])
    mid_out[...] = merge([mid_part[0]] + [mid_got[i] for i in range(3)])
    for d in range(8):
        tl = lax.rem(zl + d, 8)
        move = hand_over(mid_out, tl * OUT_ROWS, zl * 3 + 1, z - zl + tl, o_s.at[1])
        if d:
            send(*move)
        else:
            pltpu.make_async_copy(move[0], move[1], o_r).start()

    landed_all(landed, o_r)
    o_ref[...] = landed[...]
    landed_all(full.at[:, pl.ds(0, 6)], y_s)
    landed_all(full, c_s)
    landed_all(full.at[0, :, pl.ds(0, 144)], x_s)
    landed_all(full_got, p_s.at[0])
    landed_all(mid_got, p_s.at[1])
    landed_all(landed.at[:, pl.ds(0, 15 * HD)], o_s.at[0])

    landed_all(landed.at[:, pl.ds(0, 7 * HD)], o_s.at[1])


def on_device(query_rows, key_rows, value_rows):
    dma = pltpu.SemaphoreType.DMA
    return pl.pallas_call(
        kernel,
        out_shape=pltpu.VMEM((OUT_ROWS, 24 * HD), BF16),
        in_specs=[pl.BlockSpec(memory_space=pl.ANY)] * 3,
        out_specs=pl.BlockSpec(memory_space=pltpu.VMEM),
        scratch_shapes=[
            pltpu.VMEM((2, 8, 256, HD), BF16),
            pltpu.VMEM((2, 8, 256, HD), BF16),
            pltpu.VMEM((4, 256, HD), BF16),
            pltpu.VMEM((4, 128, HD), BF16),
            pltpu.VMEM((8, HD, 256), BF16),
            pltpu.VMEM((8, HD, 256), BF16),
            pltpu.VMEM((8, 256, 256), F32),
            pltpu.VMEM((2, 8, 256, 256), BF16),
            pltpu.VMEM((4, HD + 8, 256), F32),
            pltpu.VMEM((4, HD + 8, 128), F32),
            pltpu.VMEM((3, HD + 8, 256), F32),
            pltpu.VMEM((3, HD + 8, 128), F32),
            pltpu.VMEM((256, HD), BF16),
            pltpu.VMEM((128, HD), BF16),
            pltpu.VMEM((OUT_ROWS, 24 * HD), BF16),
            dma((5,)), dma((5,)),
            dma(()), dma((6, 3)),
            dma(()), dma((6,)),
            dma(()), dma((2,)),
            dma((2,)), dma((2,)),
            dma((2,)), dma(()), dma(()),
        ],
        compiler_params=pltpu.CompilerParams(
            collective_id=0, has_side_effects=True, vmem_limit_bytes=60 * 2**20
        ),
        name="attend",
    )(query_rows, key_rows, value_rows)


def solution(mesh):
    return jax.shard_map(
        on_device,
        mesh=mesh,
        in_specs=(P("blk", "ulysses"), P("blk", "ulysses"), P("blk", "ulysses")),
        out_specs=P(("blk", "ulysses"), None),
        check_vma=False,
    )
```

time: 57.7 us -> 53 us (0.919)
  the two profiles are of different devices: /device:TPU:2 before, /device:TPU:1 now
where the time goes in v3:
time: 53 us; the launch traced here: 52.9 us
  Pallas kernels  52.3 us (99%)
  local copies, waits for them, and re-layouts  0.64 us (1%)
    pallas_call x1, Pallas kernels, on_device(): pl.pallas_call(kernel, out_shape=pltpu.VMEM((OUT_ROWS, 24 * HD), BF16), i...  52.3 us

profile of v3, /device:TPU:1, one launch (start us, length us, event | category | flops | bytes accessed | tf_op | source)
XLA Modules:
  0.0 52.9 jit_solution(449853770137759526)
XLA Ops:
  0.0 52.3 %attend.1 = bf16[16,3072]{1,0:T(8,128)(2,1)S(1)} custom-call(bf16[128,384]{1,0:T(8,128)(2,1)} %q_ref.1, bf16[128,384]{1,0:T(8,128)(2,1)} %k_ref.1, bf16[128,384]{1,0:T(8,128)(2,1)} %v_ref.1), custom_call_target="tpu_custom_call" | custom-call | tf_op jit(solution)/shard_map/attend/pallas_call | solution.py:284
  52.3 0.6 %copy.5 = bf16[16,3072]{1,0:T(8,128)(2,1)} copy(bf16[16,3072]{1,0:T(8,128)(2,1)S(1)} %attend.1) | data formatting | bytes 196608

commit v4 on v3

--- a/solution.py
+++ b/solution.py
@@ -57,7 +57,7 @@
     q_ref, k_ref, v_ref, o_ref,
     full, mid, full_q, mid_q, full_vt, mid_vt, scores, weights,
     full_part, mid_part, full_got, mid_got, full_out, mid_out, landed,
-    z_s, z_r, y_s, y_r, c_s, c_r, x_s, x_r, p_s, p_r, o_s, o_r, l_s,
+    z_s, z_r, y_s, y_r, c_s, c_r, x_s, x_r, p_s, p_r, o_s, o_r, l_s, met,
 ):
     b = lax.axis_index("blk")
     zl = lax.axis_index("ulysses")
@@ -89,6 +89,9 @@
         pl.semaphore_signal(barrier, inc=1, device_id=peer, device_id_type=MESH)
     pl.semaphore_wait(barrier, len(peers))
 
+    for d in (4, 12):
+        pl.semaphore_signal(met, inc=1, device_id=at(dz=d), device_id_type=MESH)
+
     held_by, queries_by = (full, mid), (full_q, mid_q)
     columns = pl.ds(HD, HD)
 
@@ -170,28 +173,28 @@
         for j in range(8):
             turned[j] = held_by[head][1, j].T
 
-    def send_part(head, d):
-        part, got = ((full_part, full_got), (mid_part, mid_got))[head]
-        send(part.at[d], got.at[d - 1], p_s.at[head], p_r.at[head], at(dx=d))
-
-    def full_tile(d):
-        q = full_q[lax.rem(x + d, 4)]
-        peak, total = weigh_tile(lambda j: full[0, j], q, scores, weights.at[0])
-        pack(full_part, d, sum_tile(lambda j: full_vt[j], weights.at[0]), peak, total)
-        if d:
-            send_part(0, d)
-
-    def mid_weigh(i, d_a, d_b):
-        q = jnp.concatenate([mid_q[lax.rem(x + d, 4)] for d in (d_a, d_b)], axis=0)
-        return weigh_tile(lambda j: mid[0, j], q, scores, weights.at[i])
-
-    def mid_sum(i, d_a, d_b, peak, total):
-        sums = sum_tile(lambda j: mid_vt[j], weights.at[i])
-        for k, d in enumerate((d_a, d_b)):
+    parts = ((full_part.at[0], full_got.at[0]), (full_part.at[1], full_got.at[1]), (mid_part, mid_got))
+
+    def weigh(group, i, pair):
+        if group == 2:
+            q = [mid_q[lax.rem(x + d, 4)] for d in pair]
+        else:
+            q = [full_q[lax.rem(x + d, 4), group * ROWS : (group + 1) * ROWS] for d in pair]
+        keys = mid if group == 2 else full
+        return weigh_tile(lambda j: keys[0, j], jnp.concatenate(q, axis=0), scores, weights.at[i])
+
+    def add_up(group, i, pair, weighed):
+        turned = mid_vt if group == 2 else full_vt
+        sums = sum_tile(lambda j: turned[j], weights.at[i])
+        for k, d in enumerate(pair):
             cut = slice(k * ROWS, (k + 1) * ROWS)
-            pack(mid_part, d, sums[:, cut], peak[:, cut], total[:, cut])
+            part, got = parts[group]
+            pack(part, d, sums[:, cut], weighed[0][:, cut], weighed[1][:, cut])
             if d:
-                send_part(1, d)
+                send(part.at[d], got.at[d - 1], p_s.at[group], p_r.at[group], at(dx=d))
+
+    def both(group, i, pair):
+        add_up(group, i, pair, weigh(group, i, pair))
 
     z_start(0)
     z_start(1)
@@ -199,6 +202,7 @@
     own_queries()
     own_block(0)
     own_block(1)
+    pl.semaphore_wait(met, 2)
     relay_block(2)
     relay_block(3)
     spread_block(0)
@@ -208,29 +212,29 @@
     spread_queries()
     relay_block(0)
     relay_block(1)
+    spread_block(4)
     wait_block(0)
     wait_block(1)
     turn_values(0, full_vt)
     wait_queries(0)
-    full_tile(2)
-    spread_block(4)
-    full_tile(1)
+    both(0, 0, (2, 1))
     spread_block(5)
-    full_tile(3)
-    full_tile(0)
+    both(0, 1, (3, 0))
+    both(1, 0, (2, 1))
     relay_block(4)
+    both(1, 1, (3, 0))
     relay_block(5)
     own_landed()
     wait_queries(1)
     wait_block(2)
     wait_block(3)
     wait_block(4)
-    first_pair = mid_weigh(0, 2, 1)
-    other_pair = mid_weigh(1, 3, 0)
+    first_pair = weigh(2, 0, (2, 1))
+    other_pair = weigh(2, 1, (3, 0))
     wait_block(5)
     turn_values(1, mid_vt)
-    mid_sum(0, 2, 1, *first_pair)
-    mid_sum(1, 3, 0, *other_pair)
+    add_up(2, 0, (2, 1), first_pair)
+    add_up(2, 1, (3, 0), other_pair)
     z_sent(0)
     z_sent(1)
     z_sent(2)
@@ -246,18 +250,26 @@
         dst = landed.at[:, pl.ds(pl.multiple_of(head * HD, HD), HD)]
         return src, dst, sem, o_r, (((x * 4 + y) * 2 + tz // 8) * 2 + c, lax.rem(tz, 8))
 
-    landed_all(full_got, p_r.at[0])
-    full_out[...] = merge([full_part[0]] + [full_got[i] for i in range(3)])
-    for d in range(16):
-        tz = lax.rem(z + d, 16)
-        s = lax.rem(first + tz // 8, 2)
-        move = hand_over(full_out, s * ROWS + lax.rem(tz, 8) * OUT_ROWS, head_base + 2 * r, tz, o_s.at[0])
-        if d:
-            send(*move)
-        else:
-            pltpu.make_async_copy(move[0], move[1], o_r).start()
-
-    landed_all(mid_got, p_r.at[1])
+    for s in range(2):
+        landed_all(full_got.at[s], p_r.at[s])
+        full_out[s * ROWS : (s + 1) * ROWS] = merge([full_part[s, 0]] + [full_got[s, i] for i in range(3)])
+        half = lax.rem(first + s, 2)
+        for d in range(8):
+            tl = lax.rem(zl + d, 8)
+            move = hand_over(full_out, s * ROWS + tl * OUT_ROWS, head_base + 2 * r, half * 8 + tl, o_s.at[0])
+            if d:
+                send(*move)
+                continue
+
+            @pl.when(half != z // 8)
+            def _():
+                send(*move)
+
+            @pl.when(half == z // 8)
+            def _():
+                pltpu.make_async_copy(move[0], move[1], o_r).start()
+
+    landed_all(mid_got, p_r.at[2])
     mid_out[...] = merge([mid_part[0]] + [mid_got[i] for i in range(3)])
     for d in range(8):
         tl = lax.rem(zl + d, 8)
@@ -272,8 +284,9 @@
     landed_all(full.at[:, pl.ds(0, 6)], y_s)
     landed_all(full, c_s)
     landed_all(full.at[0, :, pl.ds(0, 144)], x_s)
-    landed_all(full_got, p_s.at[0])
-    landed_all(mid_got, p_s.at[1])
+    landed_all(full_got.at[0], p_s.at[0])
+    landed_all(full_got.at[1], p_s.at[1])
+    landed_all(mid_got, p_s.at[2])
     landed_all(landed.at[:, pl.ds(0, 15 * HD)], o_s.at[0])
 
     landed_all(landed.at[:, pl.ds(0, 7 * HD)], o_s.at[1])
@@ -295,9 +308,9 @@
             pltpu.VMEM((8, HD, 256), BF16),
             pltpu.VMEM((8, 256, 256), F32),
             pltpu.VMEM((2, 8, 256, 256), BF16),
-            pltpu.VMEM((4, HD + 8, 256), F32),
+            pltpu.VMEM((2, 4, HD + 8, 128), F32),
             pltpu.VMEM((4, HD + 8, 128), F32),
-            pltpu.VMEM((3, HD + 8, 256), F32),
+            pltpu.VMEM((2, 3, HD + 8, 128), F32),
             pltpu.VMEM((3, HD + 8, 128), F32),
             pltpu.VMEM((256, HD), BF16),
             pltpu.VMEM((128, HD), BF16),
@@ -306,8 +319,8 @@
             dma(()), dma((6, 3)),
             dma(()), dma((6,)),
             dma(()), dma((2,)),
-            dma((2,)), dma((2,)),
-            dma((2,)), dma(()), dma(()),
+            dma((3,)), dma((3,)),
+            dma((2,)), dma(()), dma(()), pltpu.SemaphoreType.REGULAR,
         ],
         compiler_params=pltpu.CompilerParams(
             collective_id=0, has_side_effects=True, vmem_limit_bytes=60 * 2**20

time: 53 us -> 52.2 us (0.985)
  Pallas kernels: 52.3 us -> 51.4 us
    pallas_call x1, Pallas kernels: 52.3 us -> 51.4 us  [on_device(): pl.pallas_call(kernel, out_shape=pltpu.VMEM((OUT_ROWS, 24 * HD), BF16), i...]
where the time goes in v4:
time: 52.2 us; the launch traced here: 52.1 us
  Pallas kernels  51.4 us (98%)
  local copies, waits for them, and re-layouts  0.64 us (1%)
    pallas_call x1, Pallas kernels, on_device(): pl.pallas_call(kernel, out_shape=pltpu.VMEM((OUT_ROWS, 24 * HD), BF16), i...  51.4 us

profile of v4, /device:TPU:1, one launch (start us, length us, event | category | flops | bytes accessed | tf_op | source)
XLA Modules:
  0.0 52.1 jit_solution(3554368545466045687)
XLA Ops:
  0.0 51.4 %attend.1 = bf16[16,3072]{1,0:T(8,128)(2,1)S(1)} custom-call(bf16[128,384]{1,0:T(8,128)(2,1)} %q_ref.1, bf16[128,384]{1,0:T(8,128)(2,1)} %k_ref.1, bf16[128,384]{1,0:T(8,128)(2,1)} %v_ref.1), custom_call_target="tpu_custom_call" | custom-call | tf_op jit(solution)/shard_map/attend/pallas_call | solution.py:297
  51.4 0.6 %copy.5 = bf16[16,3072]{1,0:T(8,128)(2,1)} copy(bf16[16,3072]{1,0:T(8,128)(2,1)S(1)} %attend.1) | data formatting | bytes 196608

commit v5 on v4

--- a/solution.py
+++ b/solution.py
@@ -208,8 +208,8 @@
     spread_block(0)
     m_start(0)
     m_start(1)
+    spread_queries()
     spread_block(1)
-    spread_queries()
     relay_block(0)
     relay_block(1)
     spread_block(4)

time: 52.2 us -> 53.7 us (1.029)
  Pallas kernels: 51.4 us -> 52.9 us
    pallas_call x1, Pallas kernels: 51.4 us -> 52.9 us  [on_device(): pl.pallas_call(kernel, out_shape=pltpu.VMEM((OUT_ROWS, 24 * HD), BF16), i...]
where the time goes in v5:
time: 53.7 us; the launch traced here: 53.6 us
  Pallas kernels  52.9 us (99%)
  local copies, waits for them, and re-layouts  0.64 us (1%)
    pallas_call x1, Pallas kernels, on_device(): pl.pallas_call(kernel, out_shape=pltpu.VMEM((OUT_ROWS, 24 * HD), BF16), i...  52.9 us

profile of v5, /device:TPU:1, one launch (start us, length us, event | category | flops | bytes accessed | tf_op | source)
XLA Modules:
  0.0 53.6 jit_solution(18303521652233464583)
XLA Ops:
  0.0 52.9 %attend.1 = bf16[16,3072]{1,0:T(8,128)(2,1)S(1)} custom-call(bf16[128,384]{1,0:T(8,128)(2,1)} %q_ref.1, bf16[128,384]{1,0:T(8,128)(2,1)} %k_ref.1, bf16[128,384]{1,0:T(8,128)(2,1)} %v_ref.1), custom_call_target="tpu_custom_call" | custom-call | tf_op jit(solution)/shard_map/attend/pallas_call | solution.py:297
  52.9 0.6 %copy.5 = bf16[16,3072]{1,0:T(8,128)(2,1)} copy(bf16[16,3072]{1,0:T(8,128)(2,1)S(1)} %attend.1) | data formatting | bytes 196608
